TPU v7x, 768 devices: a whole 4x8x12 slice. The times are simulated.
768 devices in a mesh: blk: 32 (over z_hi, y, core), group: 24 (over x, z_lo).
Axes of the slice: x: 4, y: 8, z: 12 (z_hi: 2, z_lo: 6; z = z_hi * 6 + z_lo), core: 2. Of those that a mesh axis runs over, the one named last changes fastest.
Arguments:
- image_embed: float32 [196608, 1152], P(('blk', 'group')), may hold values from -2.5 to 2.5
- text_embed: float32 [196608, 1152], P(('blk', 'group')), may hold values from -2.5 to 2.5
- logit_scale: float32 [1], replicated, may hold values from 2 to 8
- logit_bias: float32 [1], replicated, may hold values from -3 to -0.5
Outputs:
- picture_vector_derivative: float32 [196608, 1152], P(('blk', 'group'))
- caption_vector_derivative: float32 [196608, 1152], P(('blk', 'group'))
- logit_scaling_derivative: float32 [1], replicated
All inputs are finite; a program needn't handle non-finite values.
Results may differ from a plain program's by a relative error of at most 0.0065.
Values may be sent and summed in bfloat16 or wider, within the bound.
A program may use at most 32 MiB of HBM per device.

v0:
```python
import jax
import jax.numpy as jnp
from jax import lax
from jax.sharding import PartitionSpec as P

HALF = 2


def shifted(shard, axis, by):
    size = lax.axis_size(axis)
    return lax.ppermute(shard, axis, [(i, (i + by) % size) for i in range(size)])


def local(image_embed, text_embed, logit_scale, logit_bias):
    temper = logit_scale[0]
    offset = logit_bias[0]
    rows = image_embed.shape[0]
    image_inv = lax.rsqrt(jnp.sum(image_embed * image_embed, axis=1, keepdims=True) + 1e-06)
    text_inv = lax.rsqrt(jnp.sum(text_embed * text_embed, axis=1, keepdims=True) + 1e-06)
    image_unit = image_embed * image_inv
    text_unit = text_embed * text_inv
    image_low = image_unit.astype(jnp.bfloat16)
    text_low = text_unit.astype(jnp.bfloat16)
    identity = jnp.eye(rows, dtype=jnp.float32)
    empty = jnp.zeros(image_unit.shape, jnp.float32)
    scale_term = jnp.zeros((), jnp.float32)
    image_dir = empty
    text = shifted(text_low, "blk", HALF)
    carried = empty
    for place in range(2 * HALF + 1):
        if place > 0:
            text = shifted(text, "blk", -1)
            carried = shifted(carried, "blk", -1)
        visit_image_dir = image_dir
        visit_scale_term = scale_term
        inner = lax.dot_general(
            image_low, text, (((1,), (1,)), ((), ())), preferred_element_type=jnp.float32
        )
        logits = temper * inner + offset
        if place == HALF:
            sign = 2.0 * identity - 1.0
        else:
            sign = -jnp.ones((rows, rows), jnp.float32)
        coeff = (-sign * jax.nn.sigmoid(-sign * logits)).astype(jnp.bfloat16)
        visit_image_dir = visit_image_dir + temper * jnp.dot(
            coeff, text, preferred_element_type=jnp.float32
        )
        term = temper * lax.dot_general(
            coeff, image_low, (((0,), (0,)), ((), ())), preferred_element_type=jnp.float32
        )
        visit_scale_term = visit_scale_term + jnp.sum(coeff.astype(jnp.float32) * inner)
        image_dir, term, scale_term = (visit_image_dir, term, visit_scale_term)
        carried = carried + term
    text_dir = shifted(carried.astype(jnp.bfloat16), "blk", HALF).astype(carried.dtype)
    picture_vector_derivative = image_inv * (
        image_dir - image_unit * jnp.sum(image_unit * image_dir, axis=1, keepdims=True)
    )
    caption_vector_derivative = text_inv * (
        text_dir - text_unit * jnp.sum(text_unit * text_dir, axis=1, keepdims=True)
    )
    overall_accumulation = lax.psum(scale_term, ("blk", "group"))
    matched_sample_number = rows * lax.axis_size("blk") * lax.axis_size("group")
    logit_scaling_derivative = jnp.reshape(overall_accumulation / matched_sample_number, (1,))
    return (picture_vector_derivative, caption_vector_derivative, logit_scaling_derivative)


def solution(mesh):
    placed = (P(("blk", "group"), None), P(("blk", "group"), None), P(), P())
    return jax.shard_map(
        local,
        mesh=mesh,
        in_specs=placed,
        out_specs=(P(("blk", "group"), None), P(("blk", "group"), None), P()),
        check_vma=False,
    )
```

profile of v0, /device:TPU:64, one launch (start us, length us, event | category | flops | bytes accessed | tf_op | source)
XLA Modules:
  0.0 457.9 jit_solution(12988220032651314006)
XLA Ops:
  0.6 1.5 multiply_reduce_fusion.1
  2.2 0.1 copy-done.1
  2.3 0.1 multiply_convert_fusion
  2.4 3.6 collective-permute-start
  6.0 0.2 multiply_reduce_fusion.2
  7.5 0.1 multiply_convert_fusion.1
  7.7 50.9 %collective-permute-done = bf16[256,1152]{1,0:T(8,128)(2,1)S(1)} collective-permute-done((bf16[256,1152]{1,0:T(8,128)(2,1)S(1)}, bf16[256,1152]{1,0:T(8,128)(2,1)S(1)}, u32[]{:S(2)}, u32[]{:S(2)}) %collective-permute-start) | collective-permute-done | bytes 589856 | tf_op jit(solution)/shard_map/ppermute | solution.py:11
  58.5 1.0 multiply_reduce_fusion.7
  59.5 0.4 convolution_multiply_fusion.4
  59.9 1.9 collective-permute-start.5
  61.9 1.9 collective-permute-start.1
  63.8 49.0 %collective-permute-done.1 = bf16[256,1152]{1,0:T(8,128)(2,1)S(1)} collective-permute-done((bf16[256,1152]{1,0:T(8,128)(2,1)S(1)}, bf16[256,1152]{1,0:T(8,128)(2,1)S(1)}, u32[]{:S(2)}, u32[]{:S(2)}) %collective-permute-start.1) | collective-permute-done | bytes 589856 | tf_op jit(solution)/shard_map/ppermute | solution.py:11
  112.8 1.0 multiply_reduce_fusion.6
  113.9 0.0 collective-permute-done.5
  113.9 0.4 fusion.1
  114.3 0.3 copy-done.5
  114.6 12.3 %collective-permute-start.6 = (f32[256,1152]{1,0:T(8,128)S(1)}, f32[256,1152]{1,0:T(8,128)S(1)}, u32[]{:S(2)}, u32[]{:S(2)}) collective-permute-start(f32[256,1152]{1,0:T(8,128)S(1)} %fusion.1), channel_id=1, source_target_pairs={{0,744},{24,0},{48,24},{72,48},{96,72},{120,96},{144,120},{168,144... | collective-permute-start | bytes 3538952 | tf_op jit(solution)/shard_map/ppermute | solution.py:11
  126.9 1.9 collective-permute-start.2
  128.8 48.3 %collective-permute-done.2 = bf16[256,1152]{1,0:T(8,128)(2,1)} collective-permute-done((bf16[256,1152]{1,0:T(8,128)(2,1)S(1)}, bf16[256,1152]{1,0:T(8,128)(2,1)}, u32[]{:S(2)}, u32[]{:S(2)}) %collective-permute-start.2) | collective-permute-done | bytes 589856 | tf_op jit(solution)/shard_map/ppermute | solution.py:11
  177.1 2.2 multiply_reduce_fusion.5
  179.3 0.4 convolution_multiply_fusion.2
  179.7 0.3 copy-done.9
  180.0 0.0 collective-permute-done.6
  180.0 1.1 add.110
  181.1 12.4 %collective-permute-start.7 = (f32[256,1152]{1,0:T(8,128)}, f32[256,1152]{1,0:T(8,128)}, u32[]{:S(2)}, u32[]{:S(2)}) collective-permute-start(f32[256,1152]{1,0:T(8,128)} %add.110), channel_id=1, source_target_pairs={{0,744},{24,0},{48,24},{72,48},{96,72},{120,96},{144,120},{168,144... | collective-permute-start | bytes 3538952 | tf_op jit(solution)/shard_map/ppermute | solution.py:11
  193.5 1.9 collective-permute-start.3
  195.4 0.4 fusion.4
  197.1 1.6 convolution_add_fusion.3
  198.7 35.5 %collective-permute-done.3 = bf16[256,1152]{1,0:T(8,128)(2,1)} collective-permute-done((bf16[256,1152]{1,0:T(8,128)(2,1)}, bf16[256,1152]{1,0:T(8,128)(2,1)}, u32[]{:S(2)}, u32[]{:S(2)}) %collective-permute-start.3) | collective-permute-done | bytes 589856 | tf_op jit(solution)/shard_map/ppermute | solution.py:11
  234.2 12.2 %collective-permute-start.4 = (bf16[256,1152]{1,0:T(8,128)(2,1)}, bf16[256,1152]{1,0:T(8,128)(2,1)S(1)}, u32[]{:S(2)}, u32[]{:S(2)}) collective-permute-start(bf16[256,1152]{1,0:T(8,128)(2,1)} %collective-permute-done.3), channel_id=1, source_target_pairs={{0,744},{24,0},{48,24},{72,48},{96,72},{120,96},{144,120},{168,144... | collective-permute-start | bytes 1769480 | tf_op jit(solution)/shard_map/ppermute | solution.py:11
  246.4 2.1 multiply_reduce_fusion.4
  248.5 0.4 convolution_multiply_fusion.1
  249.0 0.3 copy-done.11
  249.3 2.4 add.111
  251.7 1.9 collective-permute-start.8
  253.7 2.5 convolution_add_fusion.2
  257.5 27.8 %collective-permute-done.4 = bf16[256,1152]{1,0:T(8,128)(2,1)S(1)} collective-permute-done((bf16[256,1152]{1,0:T(8,128)(2,1)}, bf16[256,1152]{1,0:T(8,128)(2,1)S(1)}, u32[]{:S(2)}, u32[]{:S(2)}) %collective-permute-start.4) | collective-permute-done | bytes 589856 | tf_op jit(solution)/shard_map/ppermute | solution.py:11
  285.3 1.7 multiply_reduce_fusion.3
  287.6 1.9 convolution_add_fusion.1
  289.5 110.5 %psum.7 = f32[]{:T(128)} all-reduce(f32[]{:T(128)S(6)} %add.116), channel_id=1, replica_groups=mesh['blk'=32,'group'=24] {'blk','group'}, use_global_device_ids=true, to_apply=%region_9.0 | all-reduce | flops 1 | bytes 8 | tf_op jit(solution)/shard_map/psum | solution.py:61
  400.7 1.6 convolution_multiply_fusion
  402.4 0.5 multiply_reduce_fusion
  402.8 1.4 add_convert_fusion
  404.2 1.9 collective-permute-start.9
  406.2 1.3 subtract_multiply_fusion
  407.4 47.7 %collective-permute-done.9 = bf16[256,1152]{1,0:T(8,128)(2,1)S(1)} collective-permute-done((bf16[256,1152]{1,0:T(8,128)(2,1)S(1)}, bf16[256,1152]{1,0:T(8,128)(2,1)S(1)}, u32[]{:S(2)}, u32[]{:S(2)}) %collective-permute-start.9) | collective-permute-done | bytes 589856 | tf_op jit(solution)/shard_map/ppermute | solution.py:11
  455.2 0.3 fusion.2
  455.5 1.3 fusion.3
  (26 shorter events, 0.1 us)
Async XLA Ops:
  0.6 1.6 copy-start.1
  2.2 3.9 copy-start
  2.4 56.1 %collective-permute-start = (bf16[256,1152]{1,0:T(8,128)(2,1)S(1)}, bf16[256,1152]{1,0:T(8,128)(2,1)S(1)}, u32[]{:S(2)}, u32[]{:S(2)}) collective-permute-start(bf16[256,1152]{1,0:T(8,128)(2,1)S(1)} %multiply_convert_fusion), channel_id=1, source_target_pairs={{0,48},{24,72},{48,96},{72,120},{96,144},{120,168},{144,192},{168,... | collective-permute-start | bytes 1769480 | tf_op jit(solution)/shard_map/ppermute | solution.py:11
  7.6 171.7 %copy-start.2 = (bf16[256,1152]{1,0:T(8,128)(2,1)}, bf16[256,1152]{1,0:T(8,128)(2,1)S(1)}, u32[]{:S(2)}) copy-start(bf16[256,1152]{1,0:T(8,128)(2,1)S(1)} %multiply_convert_fusion.1) | copy-start | bytes 1769476
  59.9 53.9 %collective-permute-start.5 = (f32[256,1152]{1,0:T(8,128)S(1)}, f32[256,1152]{1,0:T(8,128)S(1)}, u32[]{:S(2)}, u32[]{:S(2)}) collective-permute-start(f32[256,1152]{1,0:T(8,128)S(1)} %convolution_multiply_fusion.4), channel_id=1, source_target_pairs={{0,744},{24,0},{48,24},{72,48},{96,72},{120,96},{144,120},{168,144... | collective-permute-start | bytes 3538952 | tf_op jit(solution)/shard_map/ppermute | solution.py:11
  61.9 51.0 %collective-permute-start.1 = (bf16[256,1152]{1,0:T(8,128)(2,1)S(1)}, bf16[256,1152]{1,0:T(8,128)(2,1)S(1)}, u32[]{:S(2)}, u32[]{:S(2)}) collective-permute-start(bf16[256,1152]{1,0:T(8,128)(2,1)S(1)} %collective-permute-done), channel_id=1, source_target_pairs={{0,744},{24,0},{48,24},{72,48},{96,72},{120,96},{144,120},{168,144... | collective-permute-start | bytes 1769480 | tf_op jit(solution)/shard_map/ppermute | solution.py:11
  112.8 14.0 %copy-start.8 = (bf16[256,1152]{1,0:T(8,128)(2,1)}, bf16[256,1152]{1,0:T(8,128)(2,1)S(1)}, u32[]{:S(2)}) copy-start(bf16[256,1152]{1,0:T(8,128)(2,1)S(1)} %collective-permute-done.1) | copy-start | bytes 1769476
  113.8 0.7 copy-start.5
  114.6 65.4 %collective-permute-start.6 = (f32[256,1152]{1,0:T(8,128)S(1)}, f32[256,1152]{1,0:T(8,128)S(1)}, u32[]{:S(2)}, u32[]{:S(2)}) collective-permute-start(f32[256,1152]{1,0:T(8,128)S(1)} %fusion.1), channel_id=1, source_target_pairs={{0,744},{24,0},{48,24},{72,48},{96,72},{120,96},{144,120},{168,144... | collective-permute-start | bytes 3538952 | tf_op jit(solution)/shard_map/ppermute | solution.py:11
  126.9 50.3 %collective-permute-start.2 = (bf16[256,1152]{1,0:T(8,128)(2,1)S(1)}, bf16[256,1152]{1,0:T(8,128)(2,1)}, u32[]{:S(2)}, u32[]{:S(2)}) collective-permute-start(bf16[256,1152]{1,0:T(8,128)(2,1)S(1)} %collective-permute-done.1), channel_id=1, source_target_pairs={{0,744},{24,0},{48,24},{72,48},{96,72},{120,96},{144,120},{168,144... | collective-permute-start | bytes 1769480 | tf_op jit(solution)/shard_map/ppermute | solution.py:11
  179.3 0.7 copy-start.9
  181.1 68.2 %collective-permute-start.7 = (f32[256,1152]{1,0:T(8,128)}, f32[256,1152]{1,0:T(8,128)}, u32[]{:S(2)}, u32[]{:S(2)}) collective-permute-start(f32[256,1152]{1,0:T(8,128)} %add.110), channel_id=1, source_target_pairs={{0,744},{24,0},{48,24},{72,48},{96,72},{120,96},{144,120},{168,144... | collective-permute-start | bytes 3538952 | tf_op jit(solution)/shard_map/ppermute | solution.py:11
  193.5 40.7 %collective-permute-start.3 = (bf16[256,1152]{1,0:T(8,128)(2,1)}, bf16[256,1152]{1,0:T(8,128)(2,1)}, u32[]{:S(2)}, u32[]{:S(2)}) collective-permute-start(bf16[256,1152]{1,0:T(8,128)(2,1)} %collective-permute-done.2), channel_id=1, source_target_pairs={{0,744},{24,0},{48,24},{72,48},{96,72},{120,96},{144,120},{168,144... | collective-permute-start | bytes 1769480 | tf_op jit(solution)/shard_map/ppermute | solution.py:11
  197.1 49.4 %copy-start.3 = (bf16[256,1152]{1,0:T(8,128)(2,1)S(1)}, bf16[256,1152]{1,0:T(8,128)(2,1)}, u32[]{:S(2)}) copy-start(bf16[256,1152]{1,0:T(8,128)(2,1)} %copy-done.2) | copy-start | bytes 1769476
  234.2 51.1 %collective-permute-start.4 = (bf16[256,1152]{1,0:T(8,128)(2,1)}, bf16[256,1152]{1,0:T(8,128)(2,1)S(1)}, u32[]{:S(2)}, u32[]{:S(2)}) collective-permute-start(bf16[256,1152]{1,0:T(8,128)(2,1)} %collective-permute-done.3), channel_id=1, source_target_pairs={{0,744},{24,0},{48,24},{72,48},{96,72},{120,96},{144,120},{168,144... | collective-permute-start | bytes 1769480 | tf_op jit(solution)/shard_map/ppermute | solution.py:11
  248.5 0.7 copy-start.11
  249.3 4.4 copy-start.10
  251.7 151.1 %collective-permute-start.8 = (f32[256,1152]{1,0:T(8,128)}, f32[256,1152]{1,0:T(8,128)}, u32[]{:S(2)}, u32[]{:S(2)}) collective-permute-start(f32[256,1152]{1,0:T(8,128)} %add.111), channel_id=1, source_target_pairs={{0,744},{24,0},{48,24},{72,48},{96,72},{120,96},{144,120},{168,144... | collective-permute-start | bytes 3538952 | tf_op jit(solution)/shard_map/ppermute | solution.py:11
  253.6 31.6 %copy-start.4 = (bf16[256,1152]{1,0:T(8,128)(2,1)S(1)}, bf16[256,1152]{1,0:T(8,128)(2,1)}, u32[]{:S(2)}) copy-start(bf16[256,1152]{1,0:T(8,128)(2,1)} %copy-done.2) | copy-start | bytes 1769476
  285.3 1.7 copy-start.6
  400.7 1.7 copy-start.7
  400.7 1.7 copy-start.12
  404.2 50.9 %collective-permute-start.9 = (bf16[256,1152]{1,0:T(8,128)(2,1)S(1)}, bf16[256,1152]{1,0:T(8,128)(2,1)S(1)}, u32[]{:S(2)}, u32[]{:S(2)}) collective-permute-start(bf16[256,1152]{1,0:T(8,128)(2,1)S(1)} %add_convert_fusion), channel_id=1, source_target_pairs={{0,48},{24,72},{48,96},{72,120},{96,144},{120,168},{144,192},{168,... | collective-permute-start | bytes 1769480 | tf_op jit(solution)/shard_map/ppermute | solution.py:11
where the time goes:
time: 459 us; the launch traced here: 458 us
  waiting for transfers between devices  259 us (56%)
  blocking collectives  111 us (24%)
  starting transfers between devices  52 us (11%)
  matrix products  18 us (4%)
  other arithmetic  9.81 us (2%)
  between operations  7.22 us (2%)
    ppermute x10, waiting for transfers between devices, shifted(): lax.ppermute(shard, axis, [(i, (i + by) % size) for i in range(size)])  259 us
    psum x1, blocking collectives, local(): overall_accumulation = lax.psum(scale_term, ('blk', 'group'))  111 us
    ppermute x10, starting transfers between devices, shifted(): lax.ppermute(shard, axis, [(i, (i + by) % size) for i in range(size)])  52 us
  transfers between devices with their start and end apart: 10, of which 6 were waited for; matrix products, arithmetic and copies ran while one was open for 4% of the time, Pallas kernels for 0%

commit v1 on v0

v1 whole, which is shorter than its diff:
```python
import functools

import jax
import jax.numpy as jnp
from jax import lax
from jax.experimental import pallas as pl
from jax.experimental.pallas import tpu as pltpu
from jax.sharding import PartitionSpec as P

MESH = pl.DeviceIdType.MESH

NY, NX, ZH, ZL = 8, 4, 2, 6
NZ = ZH * ZL

UP, DN, SIB, FWD, RELAY, OWN = range(6)
IMG, TXT = 0, 1

CHUNKS = 4
DIRECT = 2
STRIP = 32


def kernel(
    scale_ref, bias_ref, image_hbm, text_hbm, image_out, text_out, scale_out,
    feat, raw, inv, acc, part, red_c, red_y, red_z, red_x,
    load_sem, out_sem, send_sem, fwd_sem, relay_sem, recv_sem, red_send, red_recv,
):
    rows, width = image_hbm.shape
    step = rows // CHUNKS
    b, g = lax.axis_index("blk"), lax.axis_index("group")
    zh, y, c = b // (2 * NY), (b // 2) % NY, b % 2
    x, zl = g // ZL, g % ZL
    z = zh * ZL + zl

    def dev(x, y, z, c):
        return ((z // ZL) * (2 * NY) + y * 2 + c, x * ZL + z % ZL)

    other_core = dev(x, y, z, 1 - c)
    far_z = (z + ZL) % NZ

    barrier = pltpu.get_barrier_semaphore()
    peers = [other_core]
    peers += [dev(x, (y + d) % NY, z, c) for d in range(1, NY)]
    peers += [dev(x, y, (z + d) % NZ, c) for d in range(1, NZ)]
    peers += [dev((x + d) % NX, y, z, c) for d in range(1, NX)]
    peers += [dev(x, (y + d) % NY, far_z, c) for d in (1, 2, NY - 1, NY - 2)]
    for peer in peers:
        pl.semaphore_signal(barrier, inc=1, device_id=peer, device_id_type=MESH)

    loads = [
        pltpu.make_async_copy(image_hbm, raw.at[IMG], load_sem.at[IMG]),
        pltpu.make_async_copy(text_hbm, raw.at[TXT], load_sem.at[TXT]),
    ]
    loads[TXT].start()
    loads[IMG].start()

    def normalize(kind):
        def strip(i, carry):
            at = pl.ds(pl.multiple_of(i * STRIP, STRIP), STRIP)
            value = raw[kind, at, :]
            scale = lax.rsqrt(jnp.sum(value * value, axis=1, keepdims=True) + 1e-06)
            inv[kind, at, :] = jnp.broadcast_to(scale, (STRIP, 128))
            feat[OWN, kind, at, :] = (value * scale).astype(jnp.bfloat16)
            return carry

        lax.fori_loop(0, rows // STRIP, strip, 0)

    def remote(src_slot, dst_slot, kind, j, send, device):
        at = pl.ds(pl.multiple_of(j * step, step), step)
        return pltpu.make_async_remote_copy(
            src_ref=feat.at[src_slot, kind, at],
            dst_ref=feat.at[dst_slot, kind, at],
            send_sem=send,
            recv_sem=recv_sem.at[dst_slot, kind, j],
            device_id=device,
            device_id_type=MESH,
        )

    def pick(cond, a, b):
        return jnp.where(cond, a, b)

    def own_sends(kind, j):
        relayed = j >= DIRECT
        seam = y == NY - 1
        hop = seam & relayed
        up_y = pick(hop, y - 1, (y + 1) % NY)
        up_z = pick(seam & jnp.logical_not(relayed), far_z, z)
        up_slot = pick(hop, RELAY, DN)
        up = remote(OWN, up_slot, kind, j, send_sem.at[0, kind, j], dev(x, up_y, up_z, c))
        seam = y == 0
        hop = seam & relayed
        dn_y = pick(hop, y + 1, (y + NY - 1) % NY)
        dn_z = pick(seam & jnp.logical_not(relayed), far_z, z)
        dn_slot = pick(hop, RELAY, UP)
        down = remote(OWN, dn_slot, kind, j, send_sem.at[1, kind, j], dev(x, dn_y, dn_z, c))
        side = remote(OWN, SIB, kind, j, send_sem.at[2, kind, j], other_core)
        return up, down, side

    def send_own(kind):
        def one(i, carry):
            j = (i + DIRECT) % CHUNKS
            for copy in own_sends(kind, j):
                copy.start()
            return carry

        lax.fori_loop(0, CHUNKS, one, 0)

    def relay_copy(kind, j):
        to_y = pick(y == NY - 2, 0, NY - 1)
        slot = pick(y == NY - 2, DN, UP)
        return remote(RELAY, slot, kind, j, relay_sem.at[kind, j], dev(x, to_y, far_z, c))

    is_relay = (y == NY - 2) | (y == 1)

    def arrived(slot, kind, j):
        remote(OWN, slot, kind, j, fwd_sem.at[kind, j], other_core).wait_recv()

    from_slot = pick(c == 0, UP, DN)
    rest_slot = pick(c == 0, DN, UP)

    def pass_on(kind):
        def one(i, carry):
            j = (i + DIRECT) % CHUNKS if False else i
            arrived(from_slot, kind, j)
            remote(from_slot, FWD, kind, j, fwd_sem.at[kind, j], other_core).start()
            return carry

        lax.fori_loop(0, CHUNKS, one, 0)

    def await_block(slot, kind):
        def one(j, carry):
            arrived(slot, kind, j)
            return carry

        lax.fori_loop(0, CHUNKS, one, 0)

    temper = scale_ref[0]
    offset = bias_ref[0]

    def pair(slot, kind, own):
        mine = 1 - kind
        inner = lax.dot_general(
            feat[OWN, mine], feat[slot, kind], (((1,), (1,)), ((), ())),
            preferred_element_type=jnp.float32,
        )
        logits = temper * inner + offset
        if own:
            r = lax.broadcasted_iota(jnp.int32, (rows, rows), 0)
            s = lax.broadcasted_iota(jnp.int32, (rows, rows), 1)
            sign = jnp.where(r == s, 1.0, -1.0)
            coeff = -sign / (1.0 + jnp.exp(sign * logits))
        else:
            coeff = 1.0 / (1.0 + jnp.exp(-logits))
        coeff = coeff.astype(jnp.bfloat16)
        term = jnp.dot(coeff, feat[slot, kind], preferred_element_type=jnp.float32)
        if own:
            acc[mine] = term
        else:
            acc[mine] += term
        if kind == TXT:
            share = coeff.astype(jnp.float32) * inner
            share = jnp.sum(share.reshape(rows // 8, 8, rows), axis=0)
            share = share[:, :128] + share[:, 128:]
            if own:
                part[...] = share
            else:
                part[...] += share

    def finish(kind):
        out = (image_out, text_out)[kind]

        def strip(i, carry):
            at = pl.ds(pl.multiple_of(i * STRIP, STRIP), STRIP)
            scale = inv[kind, at, :][:, :1]
            unit = raw[kind, at, :] * scale
            direction = temper * acc[kind, at, :]
            along = jnp.sum(unit * direction, axis=1, keepdims=True)
            acc[kind, at, :] = scale * (direction - unit * along)
            return carry

        lax.fori_loop(0, rows // STRIP, strip, 0)
        pltpu.make_async_copy(acc.at[kind], out, out_sem.at[kind]).start()

    def reduce_over(buf, n, me, at, base):
        buf[me] = part[...]
        copies = []
        for d in range(1, n):
            copy = pltpu.make_async_remote_copy(
                src_ref=part,
                dst_ref=buf.at[me],
                send_sem=red_send.at[base + d - 1],
                recv_sem=red_recv.at[base + d - 1],
                device_id=at((me + d) % n),
                device_id_type=MESH,
            )
            copy.start()
            copies.append(copy)
        for copy in copies:
            copy.wait()
        total = buf[0]
        for i in range(1, n):
            total = total + buf[i]
        part[...] = total
        return base + n - 1

    loads[TXT].wait()
    normalize(TXT)
    pl.semaphore_wait(barrier, len(peers))
    send_own(TXT)
    loads[IMG].wait()
    normalize(IMG)
    send_own(IMG)

    @pl.when(is_relay)
    def _():
        for kind in (TXT, IMG):
            for j in range(DIRECT, CHUNKS):
                arrived(RELAY, kind, j)
                relay_copy(kind, j).start()

    pair(OWN, TXT, True)
    pair(OWN, IMG, True)

    def others(kind):
        await_block(SIB, kind)
        pair(SIB, kind, False)
        pass_on(kind)
        pair(from_slot, kind, False)

        def one(i, carry):
            slot = pick(i == 0, rest_slot, FWD)
            await_block(slot, kind)
            pair(slot, kind, False)
            return carry

        lax.fori_loop(0, 2, one, 0)

    others(TXT)
    finish(IMG)
    base = reduce_over(red_c, 2, c, lambda i: dev(x, y, z, i), 0)
    base = reduce_over(red_y, NY, y, lambda i: dev(x, i, z, c), base)
    base = reduce_over(red_x, NX, x, lambda i: dev(i, y, z, c), base)
    base = reduce_over(red_z, NZ, z, lambda i: dev(x, y, i, c), base)
    scale_out[0] = jnp.sum(part[...]) / (rows * NX * NY * NZ * 2)
    others(IMG)
    finish(TXT)

    for kind in (TXT, IMG):
        def done(j, carry, kind=kind):
            for copy in own_sends(kind, j):
                copy.wait_send()
            remote(from_slot, FWD, kind, j, fwd_sem.at[kind, j], other_core).wait_send()
            return carry

        lax.fori_loop(0, CHUNKS, done, 0)

    @pl.when(is_relay)
    def _():
        for kind in (TXT, IMG):
            for j in range(DIRECT, CHUNKS):
                relay_copy(kind, j).wait_send()

    for kind in (IMG, TXT):
        pltpu.make_async_copy(acc.at[kind], (image_out, text_out)[kind], out_sem.at[kind]).wait()


def local(image_embed, text_embed, logit_scale, logit_bias):
    rows, width = image_embed.shape
    whole = jax.ShapeDtypeStruct((rows, width), jnp.float32)
    n_red = 1 + (NY - 1) + (NX - 1) + (NZ - 1)
    return pl.pallas_call(
        kernel,
        name="window_loss",
        out_shape=(whole, whole, jax.ShapeDtypeStruct((1,), jnp.float32)),
        in_specs=[
            pl.BlockSpec(memory_space=pltpu.SMEM),
            pl.BlockSpec(memory_space=pltpu.SMEM),
            pl.BlockSpec(memory_space=pl.ANY),
            pl.BlockSpec(memory_space=pl.ANY),
        ],
        out_specs=(
            pl.BlockSpec(memory_space=pl.ANY),
            pl.BlockSpec(memory_space=pl.ANY),
            pl.BlockSpec(memory_space=pltpu.SMEM),
        ),
        scratch_shapes=[
            pltpu.VMEM((6, 2, rows, width), jnp.bfloat16),
            pltpu.VMEM((2, rows, width), jnp.float32),
            pltpu.VMEM((2, rows, 128), jnp.float32),
            pltpu.VMEM((2, rows, width), jnp.float32),
            pltpu.VMEM((8, 128), jnp.float32),
            pltpu.VMEM((2, 8, 128), jnp.float32),
            pltpu.VMEM((NY, 8, 128), jnp.float32),
            pltpu.VMEM((NZ, 8, 128), jnp.float32),
            pltpu.VMEM((NX, 8, 128), jnp.float32),
            pltpu.SemaphoreType.DMA((2,)),
            pltpu.SemaphoreType.DMA((2,)),
            pltpu.SemaphoreType.DMA((3, 2, CHUNKS)),
            pltpu.SemaphoreType.DMA((2, CHUNKS)),
            pltpu.SemaphoreType.DMA((2, CHUNKS)),
            pltpu.SemaphoreType.DMA((5, 2, CHUNKS)),
            pltpu.SemaphoreType.DMA((n_red,)),
            pltpu.SemaphoreType.DMA((n_red,)),
        ],
        compiler_params=pltpu.CompilerParams(
            collective_id=0, has_side_effects=True, vmem_limit_bytes=48 * 2**20
        ),
        cost_estimate=pl.CostEstimate(
            flops=20 * 2 * rows * rows * width,
            bytes_accessed=4 * 4 * rows * width,
            transcendentals=10 * rows * rows,
        ),
    )(logit_scale, logit_bias, image_embed, text_embed)


def solution(mesh):
    placed = (P(("blk", "group"), None), P(("blk", "group"), None), P(), P())
    return jax.shard_map(
        local,
        mesh=mesh,
        in_specs=placed,
        out_specs=(P(("blk", "group"), None), P(("blk", "group"), None), P()),
        check_vma=False,
    )
```

time: 459 us -> 97.7 us (0.21)
  the two profiles are of different devices: /device:TPU:64 before, /device:TPU:1 now
where the time goes in v1:
time: 97.7 us; the launch traced here: 97.5 us
  Pallas kernels  89.2 us (91%)
  local copies, waits for them, and re-layouts  4.56 us (5%)
  between operations  3.7 us (4%)
    pallas_call x1, Pallas kernels, local(): pl.pallas_call(kernel, name='window_loss', out_shape=(whole, whole, jax.S...  89.2 us
    unnamed x6, local copies, waits for them, and re-layouts  4.56 us

profile of v1, /device:TPU:1, one launch (start us, length us, event | category | flops | bytes accessed | tf_op | source)
XLA Modules:
  0.0 97.5 jit_solution(11142977295662733262)
XLA Ops:
  1.9 0.0 copy-start
  1.9 1.3 %copy-done = f32[256,1152]{1,0:T(8,128)S(1)} copy-done((f32[256,1152]{1,0:T(8,128)S(1)}, f32[256,1152]{1,0:T(8,128)}, u32[]{:S(2)}) %copy-start) | copy-done | bytes 1179672
  3.2 0.0 copy-start.1
  3.2 1.3 %copy-done.1 = f32[256,1152]{1,0:T(8,128)S(1)} copy-done((f32[256,1152]{1,0:T(8,128)S(1)}, f32[256,1152]{1,0:T(8,128)}, u32[]{:S(2)}) %copy-start.1) | copy-done | bytes 1179672
  4.5 89.2 %window_loss.1 = (f32[256,1152]{1,0:T(8,128)S(1)}, f32[256,1152]{1,0:T(8,128)S(1)}, f32[1]{0:T(128)}) custom-call(f32[1]{0:T(128)S(6)} %copy.10.scale_ref, f32[1]{0:T(128)S(6)} %copy.11.bias_ref, f32[256,1152]{1,0:T(8,128)S(1)} %copy-done, f32[256,1152]{1,0:T(8,128)S(1)} %copy-done.1), custom_call_target="tpu_custom_call" | custom-call | flops 3019898880 | bytes 4718592 | tf_op jit(solution)/shard_map/window_loss/pallas_call | solution.py:271
  93.7 1.0 %copy.12 = f32[256,1152]{1,0:T(8,128)} copy(f32[256,1152]{1,0:T(8,128)S(1)} %get-tuple-element.6) | data formatting | bytes 2359296
  94.7 1.0 %copy.13 = f32[256,1152]{1,0:T(8,128)} copy(f32[256,1152]{1,0:T(8,128)S(1)} %get-tuple-element.7) | data formatting | bytes 2359296
Async XLA Ops:
  1.9 1.3 %copy-start = (f32[256,1152]{1,0:T(8,128)S(1)}, f32[256,1152]{1,0:T(8,128)}, u32[]{:S(2)}) copy-start(f32[256,1152]{1,0:T(8,128)} %image_hbm.1) | copy-start | bytes 3538948
  3.2 1.3 %copy-start.1 = (f32[256,1152]{1,0:T(8,128)S(1)}, f32[256,1152]{1,0:T(8,128)}, u32[]{:S(2)}) copy-start(f32[256,1152]{1,0:T(8,128)} %text_hbm.1) | copy-start | bytes 3538948

commit v2 on v1

--- a/solution.py
+++ b/solution.py
@@ -22,8 +22,8 @@
 
 def kernel(
     scale_ref, bias_ref, image_hbm, text_hbm, image_out, text_out, scale_out,
-    feat, raw, inv, acc, part, red_c, red_y, red_z, red_x,
-    load_sem, out_sem, send_sem, fwd_sem, relay_sem, recv_sem, red_send, red_recv,
+    feat, raw, inv, acc, part, sum_c, sum_x, sum_y, sum_z, red_c, red_y, red_z, red_x, red_b,
+    load_sem, out_sem, send_sem, fwd_sem, relay_sem, recv_sem, red_send, red_recv, turn_sem,
 ):
     rows, width = image_hbm.shape
     step = rows // CHUNKS
@@ -38,14 +38,58 @@
     other_core = dev(x, y, z, 1 - c)
     far_z = (z + ZL) % NZ
 
+    home = 2 + x
+    at_home = y == home
+    at_top, at_bottom = y == NY - 1, y == 0
+    on_seam = at_top | at_bottom
+    is_relay = (y == NY - 2) | (y == 1)
     barrier = pltpu.get_barrier_semaphore()
-    peers = [other_core]
-    peers += [dev(x, (y + d) % NY, z, c) for d in range(1, NY)]
-    peers += [dev(x, y, (z + d) % NZ, c) for d in range(1, NZ)]
-    peers += [dev((x + d) % NX, y, z, c) for d in range(1, NX)]
-    peers += [dev(x, (y + d) % NY, far_z, c) for d in (1, 2, NY - 1, NY - 2)]
-    for peer in peers:
-        pl.semaphore_signal(barrier, inc=1, device_id=peer, device_id_type=MESH)
+
+    def greet(device):
+        pl.semaphore_signal(barrier, inc=1, device_id=device, device_id_type=MESH)
+
+    @pl.when(on_seam)
+    def _():
+        greet(dev(x, NY - 1 - y, far_z, c))
+        greet(dev(x, jnp.where(at_top, 1, NY - 2), far_z, c))
+
+    @pl.when(is_relay)
+    def _():
+        greet(dev(x, jnp.where(y == 1, NY - 1, 0), far_z, c))
+
+    @pl.when(on_seam | is_relay)
+    def _():
+        greet(dev(x, y, (z + 2) % NZ, c))
+        greet(dev(x, y, (z + NZ - 2) % NZ, c))
+
+    @pl.when(at_home)
+    def _():
+        for d in range(1, NZ):
+            greet(dev(x, y, (z + d) % NZ, c))
+        for d in range(1, NY):
+            greet(dev(x, (y + d) % NY, z, c))
+
+    @pl.when(jnp.logical_not(at_home))
+    def _():
+        greet(dev(x, home, z, c))
+
+    @pl.when(jnp.logical_not(at_top))
+    def _():
+        greet(dev(x, (y + 1) % NY, z, c))
+
+    @pl.when(jnp.logical_not(at_bottom))
+    def _():
+        greet(dev(x, (y + NY - 1) % NY, z, c))
+
+    greet(other_core)
+    for d in range(1, NX):
+        greet(dev((x + d) % NX, y, z, c))
+    n_greet = (
+        NX
+        + jnp.where(on_seam, 5, 2)
+        + jnp.where(is_relay, 3, 0)
+        + jnp.where(at_home, NZ + NY - 2, 1)
+    )
 
     loads = [
         pltpu.make_async_copy(image_hbm, raw.at[IMG], load_sem.at[IMG]),
@@ -79,39 +123,60 @@
     def pick(cond, a, b):
         return jnp.where(cond, a, b)
 
-    def own_sends(kind, j):
-        relayed = j >= DIRECT
-        seam = y == NY - 1
-        hop = seam & relayed
-        up_y = pick(hop, y - 1, (y + 1) % NY)
-        up_z = pick(seam & jnp.logical_not(relayed), far_z, z)
-        up_slot = pick(hop, RELAY, DN)
-        up = remote(OWN, up_slot, kind, j, send_sem.at[0, kind, j], dev(x, up_y, up_z, c))
-        seam = y == 0
-        hop = seam & relayed
-        dn_y = pick(hop, y + 1, (y + NY - 1) % NY)
-        dn_z = pick(seam & jnp.logical_not(relayed), far_z, z)
-        dn_slot = pick(hop, RELAY, UP)
-        down = remote(OWN, dn_slot, kind, j, send_sem.at[1, kind, j], dev(x, dn_y, dn_z, c))
-        side = remote(OWN, SIB, kind, j, send_sem.at[2, kind, j], other_core)
-        return up, down, side
-
-    def send_own(kind):
+    def seam_send(kind, j):
+        hop = j >= DIRECT
+        to_y = pick(hop, pick(at_top, NY - 2, 1), pick(at_top, 0, NY - 1))
+        to_z = pick(hop, z, far_z)
+        slot = pick(hop, RELAY, pick(at_top, DN, UP))
+        return remote(OWN, slot, kind, j, send_sem.at[0, kind, j], dev(x, to_y, to_z, c))
+
+    def up_send(kind, j):
+        return remote(OWN, DN, kind, j, send_sem.at[0, kind, j], dev(x, (y + 1) % NY, z, c))
+
+    def down_send(kind, j):
+        return remote(OWN, UP, kind, j, send_sem.at[1, kind, j], dev(x, (y + NY - 1) % NY, z, c))
+
+    def plain_send(kind, j):
+        slot = pick(at_top, UP, DN)
+        to_y = pick(at_top, NY - 2, 1)
+        return remote(OWN, slot, kind, j, send_sem.at[1, kind, j], dev(x, to_y, z, c))
+
+    def side_send(kind, j):
+        return remote(OWN, SIB, kind, j, send_sem.at[2, kind, j], other_core)
+
+    def each(n, action):
         def one(i, carry):
-            j = (i + DIRECT) % CHUNKS
-            for copy in own_sends(kind, j):
-                copy.start()
-            return carry
-
-        lax.fori_loop(0, CHUNKS, one, 0)
+            action(i)
+            return carry
+
+        lax.fori_loop(0, n, one, 0)
+
+    def send_legs(kind):
+        @pl.when(on_seam)
+        def _():
+            for j in range(DIRECT, CHUNKS):
+                seam_send(kind, j).start()
+
+    def send_plain(kind):
+        def one(j):
+            @pl.when(on_seam)
+            def _():
+                plain_send(kind, j).start()
+
+            @pl.when(jnp.logical_not(on_seam))
+            def _():
+                up_send(kind, j).start()
+                down_send(kind, j).start()
+
+            side_send(kind, j).start()
+
+        each(CHUNKS, one)
 
     def relay_copy(kind, j):
         to_y = pick(y == NY - 2, 0, NY - 1)
         slot = pick(y == NY - 2, DN, UP)
         return remote(RELAY, slot, kind, j, relay_sem.at[kind, j], dev(x, to_y, far_z, c))
 
-    is_relay = (y == NY - 2) | (y == 1)
-
     def arrived(slot, kind, j):
         remote(OWN, slot, kind, j, fwd_sem.at[kind, j], other_core).wait_recv()
 
@@ -120,7 +185,7 @@
 
     def pass_on(kind):
         def one(i, carry):
-            j = (i + DIRECT) % CHUNKS if False else i
+            j = i
             arrived(from_slot, kind, j)
             remote(from_slot, FWD, kind, j, fwd_sem.at[kind, j], other_core).start()
             return carry
@@ -181,84 +246,172 @@
         lax.fori_loop(0, rows // STRIP, strip, 0)
         pltpu.make_async_copy(acc.at[kind], out, out_sem.at[kind]).start()
 
-    def reduce_over(buf, n, me, at, base):
-        buf[me] = part[...]
-        copies = []
-        for d in range(1, n):
-            copy = pltpu.make_async_remote_copy(
-                src_ref=part,
-                dst_ref=buf.at[me],
-                send_sem=red_send.at[base + d - 1],
-                recv_sem=red_recv.at[base + d - 1],
-                device_id=at((me + d) % n),
-                device_id_type=MESH,
-            )
-            copy.start()
-            copies.append(copy)
-        for copy in copies:
-            copy.wait()
+    def total_of(buf, n):
         total = buf[0]
         for i in range(1, n):
             total = total + buf[i]
-        part[...] = total
-        return base + n - 1
-
-    loads[TXT].wait()
-    normalize(TXT)
-    pl.semaphore_wait(barrier, len(peers))
-    send_own(TXT)
-    loads[IMG].wait()
-    normalize(IMG)
-    send_own(IMG)
-
-    @pl.when(is_relay)
-    def _():
-        for kind in (TXT, IMG):
+        return total
+
+    def share_copy(src, buf, at, k, device):
+        return pltpu.make_async_remote_copy(
+            src_ref=src, dst_ref=buf.at[at], send_sem=red_send.at[k], recv_sem=red_recv.at[k],
+            device_id=device, device_id_type=MESH,
+        )
+
+    def reduce_over(src, dst, buf, n, me, at, base):
+        buf[me] = src[...]
+        copies = [share_copy(src, buf, me, base + d, at((me + d) % n)) for d in range(1, n)]
+        for copy in copies:
+            copy.start()
+        for copy in copies:
+            copy.wait()
+        dst[...] = total_of(buf, n)
+
+    K_C, K_X, K_Y, K_Z, K_B = 0, 2, 2 + NX, 2 + NX + NY, 2 + NX + NY + NZ
+
+    def gather_copy():
+        return share_copy(sum_x, red_y, y, K_Y + y, dev(x, home, z, c))
+
+    def spread_copy(to):
+        return share_copy(sum_z, red_b, 0, K_B + to, dev(x, to, z, c))
+
+    def home_sums():
+        red_y[y] = sum_x[...]
+        for d in range(1, NY):
+            k = (y + d) % NY
+            share_copy(sum_x, red_y, k, K_Y + k, other_core).wait_recv()
+        sum_y[...] = total_of(red_y, NY)
+        reduce_over(sum_y, sum_z, red_z, NZ, z, lambda i: dev(x, y, i, c), K_Z)
+        for d in range(1, NY):
+            spread_copy((y + d) % NY).start()
+
+    with jax.named_scope("text_load"):
+        loads[TXT].wait()
+        normalize(TXT)
+    with jax.named_scope("greeting"):
+        pl.semaphore_wait(barrier, n_greet)
+    with jax.named_scope("sends"):
+        send_legs(TXT)
+        loads[IMG].wait()
+        normalize(IMG)
+        send_legs(IMG)
+        send_plain(TXT)
+
+    phase = (z // 2) % 3
+    after = dev(x, y, (z + 2) % NZ, c)
+
+    def take_turn(kind):
+        def await_turn():
+            pl.semaphore_wait(turn_sem, 1)
+
+        def pass_turn():
+            pl.semaphore_signal(turn_sem, inc=1, device_id=after, device_id_type=MESH)
+
+        @pl.when(on_seam | is_relay)
+        def _():
+            if kind == TXT:
+                pl.when(phase > 0)(await_turn)
+            else:
+                await_turn()
+
+        @pl.when(on_seam)
+        def _():
+            for j in range(DIRECT):
+                seam_send(kind, j).start()
+            seam_send(kind, 0).wait_send()
+
+        @pl.when(is_relay)
+        def _():
             for j in range(DIRECT, CHUNKS):
                 arrived(RELAY, kind, j)
                 relay_copy(kind, j).start()
-
-    pair(OWN, TXT, True)
+            relay_copy(kind, DIRECT).wait_send()
+
+        @pl.when(on_seam | is_relay)
+        def _():
+            if kind == TXT:
+                pass_turn()
+            else:
+                pl.when(phase < 2)(pass_turn)
+
+    pl.when(phase == 0)(lambda: take_turn(TXT))
+    with jax.named_scope("own_pair"):
+        pair(OWN, TXT, True)
+    pl.when(phase > 0)(lambda: take_turn(TXT))
     pair(OWN, IMG, True)
 
     def others(kind):
-        await_block(SIB, kind)
-        pair(SIB, kind, False)
-        pass_on(kind)
-        pair(from_slot, kind, False)
+        with jax.named_scope("sibling"):
+            await_block(SIB, kind)
+            pair(SIB, kind, False)
+        with jax.named_scope("pass_on"):
+            pass_on(kind)
+        with jax.named_scope("passed_pair"):
+            pair(from_slot, kind, False)
 
         def one(i, carry):
             slot = pick(i == 0, rest_slot, FWD)
-            await_block(slot, kind)
+            with jax.named_scope("wait"):
+                await_block(slot, kind)
             pair(slot, kind, False)
             return carry
 
-        lax.fori_loop(0, 2, one, 0)
+        with jax.named_scope("rest"):
+            lax.fori_loop(0, 2, one, 0)
 
     others(TXT)
+    reduce_over(part, sum_c, red_c, 2, c, lambda i: dev(x, y, z, i), K_C)
+    reduce_over(sum_c, sum_x, red_x, NX, x, lambda i: dev(i, y, z, c), K_X)
+
+    @pl.when(jnp.logical_not(at_home))
+    def _():
+        gather_copy().start()
+
+    send_plain(IMG)
+    take_turn(IMG)
+
+    @pl.when(at_home)
+    def _():
+        home_sums()
+
     finish(IMG)
-    base = reduce_over(red_c, 2, c, lambda i: dev(x, y, z, i), 0)
-    base = reduce_over(red_y, NY, y, lambda i: dev(x, i, z, c), base)
-    base = reduce_over(red_x, NX, x, lambda i: dev(i, y, z, c), base)
-    base = reduce_over(red_z, NZ, z, lambda i: dev(x, y, i, c), base)
-    scale_out[0] = jnp.sum(part[...]) / (rows * NX * NY * NZ * 2)
     others(IMG)
-    finish(TXT)
-
-    for kind in (TXT, IMG):
-        def done(j, carry, kind=kind):
-            for copy in own_sends(kind, j):
-                copy.wait_send()
-            remote(from_slot, FWD, kind, j, fwd_sem.at[kind, j], other_core).wait_send()
-            return carry
-
-        lax.fori_loop(0, CHUNKS, done, 0)
-
-    @pl.when(is_relay)
-    def _():
+    with jax.named_scope("finish_text"):
+        finish(TXT)
+
+    scaled = 1.0 / (rows * NX * NY * NZ * 2)
+
+    @pl.when(at_home)
+    def _():
+        scale_out[0] = jnp.sum(sum_z[...]) * scaled
+        for d in range(1, NY):
+            spread_copy((y + d) % NY).wait_send()
+
+    @pl.when(jnp.logical_not(at_home))
+    def _():
+        spread_copy(y).wait_recv()
+        scale_out[0] = jnp.sum(red_b[0]) * scaled
+        gather_copy().wait_send()
+
+    with jax.named_scope("sent"):
+        def sent(n, kind, j):
+            remote(OWN, SIB, kind, j, send_sem.at[n, kind, j], other_core).wait_send()
+
         for kind in (TXT, IMG):
-            for j in range(DIRECT, CHUNKS):
-                relay_copy(kind, j).wait_send()
+            for j in range(CHUNKS):
+                sent(1, kind, j)
+                sent(2, kind, j)
+                remote(from_slot, FWD, kind, j, fwd_sem.at[kind, j], other_core).wait_send()
+                if j == 0:
+                    pl.when(jnp.logical_not(on_seam))(lambda: sent(0, kind, 0))
+                else:
+                    sent(0, kind, j)
+
+        @pl.when(is_relay)
+        def _():
+            for kind in (TXT, IMG):
+                for j in range(DIRECT + 1, CHUNKS):
+                    relay_copy(kind, j).wait_send()
 
     for kind in (IMG, TXT):
         pltpu.make_async_copy(acc.at[kind], (image_out, text_out)[kind], out_sem.at[kind]).wait()
@@ -267,7 +420,7 @@
 def local(image_embed, text_embed, logit_scale, logit_bias):
     rows, width = image_embed.shape
     whole = jax.ShapeDtypeStruct((rows, width), jnp.float32)
-    n_red = 1 + (NY - 1) + (NX - 1) + (NZ - 1)
+    n_red = 2 + NX + 2 * NY + NZ
     return pl.pallas_call(
         kernel,
         name="window_loss",
@@ -288,11 +441,12 @@
             pltpu.VMEM((2, rows, width), jnp.float32),
             pltpu.VMEM((2, rows, 128), jnp.float32),
             pltpu.VMEM((2, rows, width), jnp.float32),
-            pltpu.VMEM((8, 128), jnp.float32),
+            *[pltpu.VMEM((8, 128), jnp.float32)] * 5,
             pltpu.VMEM((2, 8, 128), jnp.float32),
             pltpu.VMEM((NY, 8, 128), jnp.float32),
             pltpu.VMEM((NZ, 8, 128), jnp.float32),
             pltpu.VMEM((NX, 8, 128), jnp.float32),
+            pltpu.VMEM((1, 8, 128), jnp.float32),
             pltpu.SemaphoreType.DMA((2,)),
             pltpu.SemaphoreType.DMA((2,)),
             pltpu.SemaphoreType.DMA((3, 2, CHUNKS)),
@@ -301,9 +455,10 @@
             pltpu.SemaphoreType.DMA((5, 2, CHUNKS)),
             pltpu.SemaphoreType.DMA((n_red,)),
             pltpu.SemaphoreType.DMA((n_red,)),
+            pltpu.SemaphoreType.REGULAR,
         ],
         compiler_params=pltpu.CompilerParams(
-            collective_id=0, has_side_effects=True, vmem_limit_bytes=48 * 2**20
+            collective_id=0, has_side_effects=True, vmem_limit_bytes=60 * 2**20
         ),
         cost_estimate=pl.CostEstimate(
             flops=20 * 2 * rows * rows * width,

time: 97.7 us -> 91.4 us (0.936)
  the two profiles are of different devices: /device:TPU:1 before, /device:TPU:321 now
where the time goes in v2:
time: 91.4 us; the launch traced here: 91.1 us
  Pallas kernels  83.9 us (92%)
  between operations  3.76 us (4%)
  local copies, waits for them, and re-layouts  3.47 us (4%)
    pallas_call x1, Pallas kernels, local(): pl.pallas_call(kernel, name='window_loss', out_shape=(whole, whole, jax.S...  83.9 us
    unnamed x4, local copies, waits for them, and re-layouts  3.47 us

profile of v2, /device:TPU:321, one launch (start us, length us, event | category | flops | bytes accessed | tf_op | source)
XLA Modules:
  0.0 91.1 jit_solution(8097280843160535759)
XLA Ops:
  1.9 83.9 %window_loss.1 = (f32[256,1152]{1,0:T(8,128)}, f32[256,1152]{1,0:T(8,128)}, f32[1]{0:T(128)}) custom-call(f32[1]{0:T(128)S(6)} %copy.10.scale_ref, f32[1]{0:T(128)S(6)} %copy.11.bias_ref, f32[256,1152]{1,0:T(8,128)} %image_hbm.1, f32[256,1152]{1,0:T(8,128)} %text_hbm.1), custom_call_target="tpu_custom_call" | custom-call | flops 3019898880 | bytes 4718592 | tf_op jit(solution)/shard_map/window_loss/pallas_call | solution.py:424
  85.8 0.0 copy-start
  85.8 2.5 %copy.12 = f32[256,1152]{1,0:T(8,128)} copy(f32[256,1152]{1,0:T(8,128)} %get-tuple-element.6) | data formatting | bytes 2359296
  88.3 0.0 copy-done
  88.3 1.0 %copy.13 = f32[256,1152]{1,0:T(8,128)} copy(f32[256,1152]{1,0:T(8,128)S(1)} %copy-done) | data formatting | bytes 2359296
Async XLA Ops:
  85.8 2.5 %copy-start = (f32[256,1152]{1,0:T(8,128)S(1)}, f32[256,1152]{1,0:T(8,128)}, u32[]{:S(2)}) copy-start(f32[256,1152]{1,0:T(8,128)} %get-tuple-element.7) | copy-start | bytes 3538948

commit v3 on v2

--- a/solution.py
+++ b/solution.py
@@ -38,7 +38,7 @@
     other_core = dev(x, y, z, 1 - c)
     far_z = (z + ZL) % NZ
 
-    home = 2 + x
+    home = 3 + x % 2
     at_home = y == home
     at_top, at_bottom = y == NY - 1, y == 0
     on_seam = at_top | at_bottom
@@ -294,8 +294,8 @@
         send_legs(TXT)
         loads[IMG].wait()
         normalize(IMG)
+        send_plain(TXT)
         send_legs(IMG)
-        send_plain(TXT)
 
     phase = (z // 2) % 3
     after = dev(x, y, (z + 2) % NZ, c)
@@ -340,26 +340,29 @@
     pl.when(phase > 0)(lambda: take_turn(TXT))
     pair(OWN, IMG, True)
 
+    crossing = (at_top & (c == 0)) | (at_bottom & (c == 1))
+
     def others(kind):
-        with jax.named_scope("sibling"):
-            await_block(SIB, kind)
-            pair(SIB, kind, False)
-        with jax.named_scope("pass_on"):
-            pass_on(kind)
-        with jax.named_scope("passed_pair"):
-            pair(from_slot, kind, False)
-
-        def one(i, carry):
-            slot = pick(i == 0, rest_slot, FWD)
-            with jax.named_scope("wait"):
-                await_block(slot, kind)
-            pair(slot, kind, False)
-            return carry
-
-        with jax.named_scope("rest"):
-            lax.fori_loop(0, 2, one, 0)
+        def rest():
+            await_block(rest_slot, kind)
+            pair(rest_slot, kind, False)
+
+        await_block(SIB, kind)
+        pair(SIB, kind, False)
+        if kind == IMG:
+            pl.when(crossing)(rest)
+        pass_on(kind)
+        pair(from_slot, kind, False)
+        if kind == IMG:
+            pl.when(jnp.logical_not(crossing))(rest)
+        else:
+            rest()
+        await_block(FWD, kind)
+        pair(FWD, kind, False)
 
     others(TXT)
+    early = is_relay & (phase < 1)
+    pl.when(early)(lambda: take_turn(IMG))
     reduce_over(part, sum_c, red_c, 2, c, lambda i: dev(x, y, z, i), K_C)
     reduce_over(sum_c, sum_x, red_x, NX, x, lambda i: dev(i, y, z, c), K_X)
 
@@ -368,14 +371,15 @@
         gather_copy().start()
 
     send_plain(IMG)
-    take_turn(IMG)
-
-    @pl.when(at_home)
-    def _():
-        home_sums()
+    pl.when(jnp.logical_not(early))(lambda: take_turn(IMG))
 
     finish(IMG)
     others(IMG)
+
+    @pl.when(at_home)
+    def _():
+        home_sums()
+
     with jax.named_scope("finish_text"):
         finish(TXT)
 

time: 91.4 us -> 90.7 us (level)
  the two profiles are of different devices: /device:TPU:321 before, /device:TPU:256 now
where the time goes in v3:
time: 90.7 us; the launch traced here: 90.5 us
  Pallas kernels  83.3 us (92%)
  between operations  3.76 us (4%)
  local copies, waits for them, and re-layouts  3.47 us (4%)
    pallas_call x1, Pallas kernels, local(): pl.pallas_call(kernel, name='window_loss', out_shape=(whole, whole, jax.S...  83.3 us
    unnamed x4, local copies, waits for them, and re-layouts  3.47 us

profile of v3, /device:TPU:256, one launch (start us, length us, event | category | flops | bytes accessed | tf_op | source)
XLA Modules:
  0.0 90.5 jit_solution(16602134080200833550)
XLA Ops:
  1.9 83.3 %window_loss.1 = (f32[256,1152]{1,0:T(8,128)}, f32[256,1152]{1,0:T(8,128)}, f32[1]{0:T(128)}) custom-call(f32[1]{0:T(128)S(6)} %copy.10.scale_ref, f32[1]{0:T(128)S(6)} %copy.11.bias_ref, f32[256,1152]{1,0:T(8,128)} %image_hbm.1, f32[256,1152]{1,0:T(8,128)} %text_hbm.1), custom_call_target="tpu_custom_call" | custom-call | flops 3019898880 | bytes 4718592 | tf_op jit(solution)/shard_map/window_loss/pallas_call | solution.py:428
  85.2 0.0 copy-start
  85.2 2.5 %copy.12 = f32[256,1152]{1,0:T(8,128)} copy(f32[256,1152]{1,0:T(8,128)} %get-tuple-element.6) | data formatting | bytes 2359296
  87.7 0.0 copy-done
  87.7 1.0 %copy.13 = f32[256,1152]{1,0:T(8,128)} copy(f32[256,1152]{1,0:T(8,128)S(1)} %copy-done) | data formatting | bytes 2359296
Async XLA Ops:
  85.2 2.5 %copy-start = (f32[256,1152]{1,0:T(8,128)S(1)}, f32[256,1152]{1,0:T(8,128)}, u32[]{:S(2)}) copy-start(f32[256,1152]{1,0:T(8,128)} %get-tuple-element.7) | copy-start | bytes 3538948

commit v4 on v3

--- a/solution.py
+++ b/solution.py
@@ -231,6 +231,8 @@
             else:
                 part[...] += share
 
+    half = rows // 2
+
     def finish(kind):
         out = (image_out, text_out)[kind]
 
@@ -243,8 +245,10 @@
             acc[kind, at, :] = scale * (direction - unit * along)
             return carry
 
-        lax.fori_loop(0, rows // STRIP, strip, 0)
-        pltpu.make_async_copy(acc.at[kind], out, out_sem.at[kind]).start()
+        for h in range(2):
+            lax.fori_loop(h * half // STRIP, (h + 1) * half // STRIP, strip, 0)
+            at = pl.ds(h * half, half)
+            pltpu.make_async_copy(acc.at[kind, at], out.at[at], out_sem.at[kind, h]).start()
 
     def total_of(buf, n):
         total = buf[0]
@@ -418,7 +422,10 @@
                     relay_copy(kind, j).wait_send()
 
     for kind in (IMG, TXT):
-        pltpu.make_async_copy(acc.at[kind], (image_out, text_out)[kind], out_sem.at[kind]).wait()
+        for h in range(2):
+            at = pl.ds(h * half, half)
+            out = (image_out, text_out)[kind]
+            pltpu.make_async_copy(acc.at[kind, at], out.at[at], out_sem.at[kind, h]).wait()
 
 
 def local(image_embed, text_embed, logit_scale, logit_bias):
@@ -452,7 +459,7 @@
             pltpu.VMEM((NX, 8, 128), jnp.float32),
             pltpu.VMEM((1, 8, 128), jnp.float32),
             pltpu.SemaphoreType.DMA((2,)),
-            pltpu.SemaphoreType.DMA((2,)),
+            pltpu.SemaphoreType.DMA((2, 2)),
             pltpu.SemaphoreType.DMA((3, 2, CHUNKS)),
             pltpu.SemaphoreType.DMA((2, CHUNKS)),
             pltpu.SemaphoreType.DMA((2, CHUNKS)),

time: 90.7 us -> 90.5 us (level)
  no operation moved by 1% of the time
where the time goes in v4:
time: 90.5 us; the launch traced here: 90.3 us
  Pallas kernels  83.1 us (92%)
  between operations  3.76 us (4%)
  local copies, waits for them, and re-layouts  3.47 us (4%)
    pallas_call x1, Pallas kernels, local(): pl.pallas_call(kernel, name='window_loss', out_shape=(whole, whole, jax.S...  83.1 us
    unnamed x4, local copies, waits for them, and re-layouts  3.47 us

profile of v4, /device:TPU:256, one launch (start us, length us, event | category | flops | bytes accessed | tf_op | source)
XLA Modules:
  0.0 90.3 jit_solution(533005910688336316)
XLA Ops:
  1.9 83.1 %window_loss.1 = (f32[256,1152]{1,0:T(8,128)}, f32[256,1152]{1,0:T(8,128)}, f32[1]{0:T(128)}) custom-call(f32[1]{0:T(128)S(6)} %copy.10.scale_ref, f32[1]{0:T(128)S(6)} %copy.11.bias_ref, f32[256,1152]{1,0:T(8,128)} %image_hbm.1, f32[256,1152]{1,0:T(8,128)} %text_hbm.1), custom_call_target="tpu_custom_call" | custom-call | flops 3019898880 | bytes 4718592 | tf_op jit(solution)/shard_map/window_loss/pallas_call | solution.py:435
  85.0 0.0 copy-start
  85.0 2.5 %copy.12 = f32[256,1152]{1,0:T(8,128)} copy(f32[256,1152]{1,0:T(8,128)} %get-tuple-element.6) | data formatting | bytes 2359296
  87.5 0.0 copy-done
  87.5 1.0 %copy.13 = f32[256,1152]{1,0:T(8,128)} copy(f32[256,1152]{1,0:T(8,128)S(1)} %copy-done) | data formatting | bytes 2359296
Async XLA Ops:
  85.0 2.5 %copy-start = (f32[256,1152]{1,0:T(8,128)S(1)}, f32[256,1152]{1,0:T(8,128)}, u32[]{:S(2)}) copy-start(f32[256,1152]{1,0:T(8,128)} %get-tuple-element.7) | copy-start | bytes 3538948
